TPU v7x, 32 devices: a whole 2x2x4 slice. The times are simulated.
32 devices in a mesh: island: 4 (over y, core), fsdp: 8 (over z, x).
Axes of the slice: x: 2, y: 2, z: 4, core: 2. Of those that a mesh axis runs over, the one named last changes fastest.
Arguments:
- tokens: bfloat16 [4, 2048, 8192], P('island', 'fsdp'), may hold values from -6 to 6
- cotangent: bfloat16 [4, 2048, 512], P('island', 'fsdp'), may hold values from -6 to 6
- key_weight: bfloat16 [4, 8192, 512], P('island', 'fsdp'), may hold values from -0.0625 to 0.0625
- quant_codes: int32 [4, 128, 8192], P('island', 'fsdp'), may hold values from 0 to 15
- zero_points: int32 [4, 128, 64], P('island', 'fsdp'), may hold values from 0 to 15
- minima: float32 [4, 128, 64], P('island', 'fsdp'), may hold values from -0.5 to 0.5
- quant_steps: float32 [4, 128, 64], P('island', 'fsdp'), may hold values from 0.01 to 0.1
- momentum: float32 [128, 8192], P('fsdp'), may hold values from -4 to 4
- params: float32 [128, 8192], P('fsdp'), may hold values from -6 to 6
Outputs:
- projected: bfloat16 [4, 2048, 512], P('island', 'fsdp')
- token_grad: bfloat16 [4, 2048, 8192], P('island', 'fsdp')
- weight_grad: float32 [4, 8192, 512], P('island', 'fsdp')
- new_momentum: float32 [128, 8192], P('fsdp')
- new_params: float32 [128, 8192], P('fsdp')
All inputs are finite; a program needn't handle non-finite values.
Results may differ from a plain program's by a relative error of at most 0.0054.
Values may be sent and summed in bfloat16 or wider, within the bound.
A program may use at most 128 MiB of HBM per device.

v0:
```python
import math

import jax
import jax.numpy as jnp
from jax import lax
from jax.sharding import PartitionSpec as P

GROUP = 128


def dequantize(quant_codes, zero_points, minima, quant_steps):
    shape = quant_codes.shape
    grouped = quant_codes.reshape(shape[:-1] + (shape[-1] // GROUP, GROUP))
    offset = (grouped - zero_points[..., None]).astype(jnp.float32)
    values = quant_steps[..., None] * offset + minima[..., None]
    return values.reshape(shape)


def local(
    tokens, cotangent, key_weight, quant_codes, zero_points, minima, quant_steps, momentum, params
):
    inputs = tokens[0]
    cot_rows = cotangent[0]
    weight = key_weight[0]
    island_tok = inputs.shape[0] * lax.axis_size("fsdp")
    scaling = 1.0 / math.sqrt(island_tok)
    piece = lax.all_gather(weight, "fsdp", axis=0, tiled=True)
    columns = inputs
    keys_acc = jnp.dot(columns, piece, preferred_element_type=jnp.float32)
    back_part = lax.dot_general(
        cot_rows, piece, (((1,), (1,)), ((), ())), preferred_element_type=jnp.float32
    )
    back_acc = back_part.astype(jnp.bfloat16)
    projected = keys_acc.astype(jnp.bfloat16)
    columns = inputs
    grad = lax.psum_scatter(
        lax.dot_general(
            columns, cot_rows, (((0,), (0,)), ((), ())), preferred_element_type=jnp.float32
        ),
        "fsdp",
        scatter_dimension=0,
        tiled=True,
    )
    weight_grad = grad * scaling
    values = dequantize(quant_codes[0], zero_points[0], minima[0], quant_steps[0])
    replicas = lax.axis_size("island")
    summed = lax.psum(values.astype(jnp.bfloat16), "island").astype(jnp.float32)
    delta = summed / replicas
    new_momentum = 0.9 * momentum + delta
    new_params = params - 0.7 * (delta + 0.9 * new_momentum)
    return (projected[None], back_acc[None], weight_grad[None], new_momentum, new_params)


def solution(mesh):
    placed = (
        P("island", "fsdp", None),
        P("island", "fsdp", None),
        P("island", "fsdp", None),
        P("island", "fsdp", None),
        P("island", "fsdp", None),
        P("island", "fsdp", None),
        P("island", "fsdp", None),
        P("fsdp", None),
        P("fsdp", None),
    )
    return jax.shard_map(
        local,
        mesh=mesh,
        in_specs=placed,
        out_specs=(
            P("island", "fsdp", None),
            P("island", "fsdp", None),
            P("island", "fsdp", None),
            P("fsdp", None),
            P("fsdp", None),
        ),
        check_vma=False,
    )
```

profile of v0, /device:TPU:0, one launch (start us, length us, event | category | flops | bytes accessed | tf_op | source)
XLA Modules:
  0.0 435.5 jit_solution(1404274721099743393)
XLA Ops:
  8.0 0.0 copy-start
  8.0 0.0 all-reduce.2.cloned.1.call-start
  8.1 0.9 add.24
  9.0 0.9 sub.17
  9.9 0.9 mul.35
  10.8 2.6 fusion.17
  13.4 0.0 all-reduce.2.cloned.1.call-update
  13.4 0.0 all-gather.3.cloned.1.call-start
  13.5 0.5 all-gather.3.cloned.1.call-update
  14.0 0.0 reduce-scatter.2.cloned.1.call-start
  14.0 0.0 copy-done
  14.1 10.3 %fusion.4 = f32[8192,512]{1,0:T(8,128)} fusion(bf16[1,256,8192]{2,1,0:T(8,128)(2,1)} %param.9, bf16[1,256,512]{2,1,0:T(8,128)(2,1)S(1)} %copy-done), kind=kOutput, calls=%fused_computation.5 | convolution fusion | flops 2147483648 | bytes 21233664 | tf_op jit(solution)/shard_map/dot_general | solution.py:37
  24.4 0.0 copy-start.3
  24.4 0.0 copy-start.4
  24.4 0.0 reduce-scatter.2.cloned.1.call-update
  24.4 24.0 %all-reduce.2.cloned.1.call-done = bf16[16,8192]{1,0:T(8,128)(2,1)} async-done(((bf16[16,8192]{1,0:T(8,128)(2,1)}), bf16[16,8192]{1,0:T(8,128)(2,1)}) %all-reduce.2.cloned.1.call-update) | async-done | bytes 262160 | tf_op jit(solution)/shard_map/psum | solution.py:47
  48.4 0.0 copy-done.3
  48.4 0.0 copy-done.4
  48.4 2.1 multiply_subtract_fusion
  50.4 92.8 %all-gather.3.cloned.1.call-done = bf16[1,8192,512]{2,1,0:T(8,128)(2,1)} async-done(((bf16[1,1024,512]{2,1,0:T(8,128)(2,1)}), bf16[1,8192,512]{2,1,0:T(8,128)(2,1)}) %all-gather.3.cloned.1.call-update) | async-done | bytes 8388624 | tf_op jit(solution)/shard_map/all_gather | solution.py:27
  143.3 0.0 copy-start.1
  143.3 0.0 copy-start.2
  143.3 7.9 %fusion = bf16[1,256,8192]{2,1,0:T(8,128)(2,1)} fusion(bf16[1,8192,512]{2,1,0:T(8,128)(2,1)} %all-gather.3.cloned.1.call-done, bf16[1,256,512]{2,1,0:T(8,128)(2,1)S(1)} %copy-done), kind=kOutput, calls=%fused_computation.1 | convolution fusion | flops 2149580800 | bytes 12845056 | tf_op jit(solution)/shard_map/dot_general | solution.py:30
  151.2 0.0 copy-done.1
  151.2 0.0 copy-done.2
  151.2 3.0 fusion.12
  154.2 270.7 %reduce-scatter.2.cloned.1.call-done = f32[1024,512]{1,0:T(8,128)} async-done(((f32[8192,512]{1,0:T(8,128)}), f32[1024,512]{1,0:T(8,128)}) %reduce-scatter.2.cloned.1.call-update) | async-done | bytes 2097168 | tf_op jit(solution)/shard_map/reduce_scatter | solution.py:36
  424.9 3.2 multiply_bitcast_fusion
Async XLA Ops:
  8.0 6.0 %copy-start = (bf16[1,256,512]{2,1,0:T(8,128)(2,1)S(1)}, bf16[1,256,512]{2,1,0:T(8,128)(2,1)}, u32[]{:S(2)}) copy-start(bf16[1,256,512]{2,1,0:T(8,128)(2,1)} %param.10) | copy-start | bytes 786436
  8.0 40.3 %all-reduce.2.cloned.1.call-start = ((), (), s32[]{:S(2)}) async-start(), calls=%async_computation.2 | async-start | bytes 524288 | tf_op jit(solution)/shard_map/psum | solution.py:47
  13.4 129.8 %all-gather.3.cloned.1.call-start = ((), (), s32[]{:S(2)}) async-start(), calls=%async_computation.3 | async-start | bytes 9437184 | tf_op jit(solution)/shard_map/all_gather | solution.py:27
  14.0 410.9 %reduce-scatter.2.cloned.1.call-start = ((), (), s32[]{:S(2)}) async-start(), calls=%async_computation.1 | async-start | bytes 18874368 | tf_op jit(solution)/shard_map/reduce_scatter | solution.py:36
  24.4 24.0 %copy-start.3 = (f32[16,8192]{1,0:T(8,128)S(1)}, f32[16,8192]{1,0:T(8,128)}, u32[]{:S(2)}) copy-start(f32[16,8192]{1,0:T(8,128)} %param.17) | copy-start | bytes 1572868
  24.4 24.0 %copy-start.4 = (f32[16,8192]{1,0:T(8,128)S(1)}, f32[16,8192]{1,0:T(8,128)}, u32[]{:S(2)}) copy-start(f32[16,8192]{1,0:T(8,128)} %param.16) | copy-start | bytes 1572868
  143.3 7.9 %copy-start.1 = (bf16[1,8192,512]{2,1,0:T(8,128)(2,1)S(1)}, bf16[1,8192,512]{2,1,0:T(8,128)(2,1)}, u32[]{:S(2)}) copy-start(bf16[1,8192,512]{2,1,0:T(8,128)(2,1)} %all-gather.3.cloned.1.call-done) | copy-start | bytes 25165828
  143.3 7.9 %copy-start.2 = (bf16[1,256,8192]{2,1,0:T(8,128)(2,1)S(1)}, bf16[1,256,8192]{2,1,0:T(8,128)(2,1)}, u32[]{:S(2)}) copy-start(bf16[1,256,8192]{2,1,0:T(8,128)(2,1)} %param.9) | copy-start | bytes 12582916
Sparse Core Ops, SparseCore 0:
  13.5 34.7 all-reduce.1
Sparse Core Ops, SparseCore 1:
  16.0 127.2 all-gather.2
  146.9 277.9 reduce-scatter.1
where the time goes:
time: 436 us; the launch traced here: 435 us
  waiting for transfers between devices  388 us (89%)
  matrix products  21.3 us (5%)
  between operations  15.5 us (4%)
  other arithmetic  7.82 us (2%)
    reduce_scatter x1, waiting for transfers between devices, local(): lax.psum_scatter(lax.dot_general(columns, cot_rows, (((0,), (0,)), ((), (...  271 us
    all_gather x1, waiting for transfers between devices, local(): piece = lax.all_gather(weight, 'fsdp', axis=0, tiled=True)  92.8 us
    psum x1, waiting for transfers between devices, local(): summed = lax.psum(values.astype(jnp.bfloat16), 'island').astype(jnp.float32)  24 us
    dot_general x1, matrix products, local(): lax.dot_general(columns, cot_rows, (((0,), (0,)), ((), ())), preferred_el...  10.3 us
  transfers between devices with their start and end apart: 3, of which 3 were waited for; matrix products, arithmetic and copies ran while one was open for 5% of the time, Pallas kernels for 0%

commit v1 on v0

v1 whole, which is shorter than its diff:
```python
import functools
import math

import jax
import jax.numpy as jnp
from jax import lax
from jax.experimental import pallas as pl
from jax.experimental.pallas import tpu as pltpu
from jax.sharding import PartitionSpec as P

GROUP = 128
MESH = pl.DeviceIdType.MESH
F32 = jnp.float32
BF16 = jnp.bfloat16
NZ = 4


def dequantize(quant_codes, zero_points, minima, quant_steps):
    shape = quant_codes.shape
    grouped = quant_codes.reshape(shape[:-1] + (shape[-1] // GROUP, GROUP))
    offset = (grouped - zero_points[..., None]).astype(F32)
    values = quant_steps[..., None] * offset + minima[..., None]
    return values.reshape(shape)


def local(
    tokens, cotangent, key_weight, quant_codes, zero_points, minima, quant_steps, momentum, params
):
    inputs = tokens[0]
    cot_rows = cotangent[0]
    weight = key_weight[0]
    island_tok = inputs.shape[0] * lax.axis_size("fsdp")
    scaling = 1.0 / math.sqrt(island_tok)
    piece = lax.all_gather(weight, "fsdp", axis=0, tiled=True)
    projected = jnp.dot(inputs, piece, preferred_element_type=F32).astype(BF16)
    back_acc = lax.dot_general(
        cot_rows, piece, (((1,), (1,)), ((), ())), preferred_element_type=F32
    ).astype(BF16)
    grad = lax.psum_scatter(
        lax.dot_general(inputs, cot_rows, (((0,), (0,)), ((), ())), preferred_element_type=F32),
        "fsdp",
        scatter_dimension=0,
        tiled=True,
    )
    weight_grad = grad * scaling
    values = dequantize(quant_codes[0], zero_points[0], minima[0], quant_steps[0])
    replicas = lax.axis_size("island")
    summed = lax.psum(values.astype(BF16), "island").astype(F32)
    delta = summed / replicas
    new_momentum = 0.9 * momentum + delta
    new_params = params - 0.7 * (delta + 0.9 * new_momentum)
    return (projected[None], back_acc[None], weight_grad[None], new_momentum, new_params)


def kernel(
    islands, rows_a, scaling,
    tok_hbm, cot_ref, w_hbm, codes_ref, zp_ref, min_ref, step_ref, mom_ref, par_ref,
    proj_ref, tg_ref, wg_ref, nmom_ref, npar_ref,
    tok, wf, part, xr_a, up_a, dn_a, up_b, dn_b, xr_b, vals, acc,
    in_sem, ga_up, ga_dn, ga_r, gax_s, gax_r, gbx, gb_up, gb_dn, gb_r,
    sax_s, sax_r, sa_s, sa_up, sa_dn, sb_s, sb_up, sb_dn, sbx, val_s, val_r,
):
    me = lax.axis_index("fsdp")
    isl = lax.axis_index("island")
    z, x = me // 2, me % 2
    ox = 1 - x
    rows = w_hbm.shape[0]
    A = pl.ds(0, rows_a)
    B = pl.ds(rows_a, rows - rows_a)
    flip = {"fsdp": me + 1 - 2 * x}
    above = {"fsdp": me + 2}
    below = {"fsdp": me - 2}
    has_up = z < NZ - 1
    has_dn = z > 0

    pending = []

    def send(make, to, cond=None):
        def copy():
            src, dst, ssem, rsem = make()
            return pltpu.make_async_remote_copy(
                src_ref=src, dst_ref=dst, send_sem=ssem, recv_sem=rsem,
                device_id=to, device_id_type=MESH)
        pending.append((cond, copy))
        copy().start()

    def arrived(dst, rsem):
        pltpu.make_async_remote_copy(
            src_ref=dst, dst_ref=dst, send_sem=rsem, recv_sem=rsem,
            device_id=flip, device_id_type=MESH).wait_recv()

    tok_in = pltpu.make_async_copy(tok_hbm, tok, in_sem.at[0])
    w_in = pltpu.make_async_copy(w_hbm, wf.at[z, x], in_sem.at[1])
    w_in.start()
    tok_in.start()

    barrier = pltpu.get_barrier_semaphore()
    pl.semaphore_signal(barrier, inc=1, device_id=flip, device_id_type=MESH)

    @pl.when(has_up)
    def _():
        pl.semaphore_signal(barrier, inc=1, device_id=above, device_id_type=MESH)

    @pl.when(has_dn)
    def _():
        pl.semaphore_signal(barrier, inc=1, device_id=below, device_id_type=MESH)

    for hop in range(1, islands):
        pl.semaphore_signal(
            barrier, inc=1, device_id={"island": (isl + hop) % islands}, device_id_type=MESH)
    pl.semaphore_wait(barrier, islands + has_up.astype(jnp.int32) + has_dn.astype(jnp.int32))

    def ga_send(zo, up, dn):
        c_up = jnp.logical_and(has_up, up)
        c_dn = jnp.logical_and(has_dn, dn)

        @pl.when(c_up)
        def _():
            send(lambda: (wf.at[zo, x, A], wf.at[zo, x, A], ga_up.at[zo], ga_r.at[zo]), above, c_up)

        @pl.when(c_dn)
        def _():
            send(lambda: (wf.at[zo, x, A], wf.at[zo, x, A], ga_dn.at[zo], ga_r.at[zo]), below, c_dn)

    def gax_send(zo, cond):
        send(lambda: (wf.at[zo, x, A], wf.at[zo, x, A], gax_s.at[zo], gax_r.at[zo]), flip, cond)

    def gb_send(zo, xo, up, dn):
        c_up = jnp.logical_and(has_up, up)
        c_dn = jnp.logical_and(has_dn, dn)

        @pl.when(c_up)
        def _():
            send(lambda: (wf.at[zo, xo, B], wf.at[zo, xo, B], gb_up.at[zo, xo], gb_r.at[zo, xo]),
                 above, c_up)

        @pl.when(c_dn)
        def _():
            send(lambda: (wf.at[zo, xo, B], wf.at[zo, xo, B], gb_dn.at[zo, xo], gb_r.at[zo, xo]),
                 below, c_dn)

    w_in.wait()
    send(lambda: (wf.at[z, x, B], wf.at[z, x, B], gbx.at[0], gbx.at[1]), flip)
    ga_send(z, True, True)

    tok_in.wait()
    cot = cot_ref[...]

    def sb_send(zt, xo, up, cond):
        if up:
            send(lambda: (part.at[zt, xo, B], up_b.at[zt, xo], sb_s.at[zt, xo], sb_up.at[zt, xo]),
                 above, cond)
        else:
            send(lambda: (part.at[zt, xo, B], dn_b.at[zt, xo], sb_s.at[zt, xo], sb_dn.at[zt, xo]),
                 below, cond)

    tile = 256
    tiles = rows // tile
    for zt in (NZ - 1, 0, 2, 1):
        def grad_tile(i, carry, zt=zt):
            xo, r = i // tiles, (i % tiles) * tile
            cols = pl.ds(pl.multiple_of((zt * 2 + xo) * rows + r, tile), tile)
            part[zt, xo, pl.ds(pl.multiple_of(r, tile), tile), :] = lax.dot_general(
                tok[:, cols], cot, (((0,), (0,)), ((), ())), preferred_element_type=F32
            ).astype(BF16)
            return carry

        lax.fori_loop(0, 2 * tiles, grad_tile, 0)
        send(lambda zt=zt: (part.at[zt, ox, A], xr_a.at[zt], sax_s.at[zt], sax_r.at[zt]), flip)
        if zt > 0:
            c0 = z == 0

            @pl.when(c0)
            def _(zt=zt):
                for xo in range(2):
                    sb_send(zt, xo, True, c0)
        if zt < NZ - 1:
            c3 = z == NZ - 1

            @pl.when(c3)
            def _(zt=zt):
                for xo in range(2):
                    sb_send(zt, xo, False, c3)

    for g in range(zp_ref.shape[1]):
        span = slice(g * GROUP, (g + 1) * GROUP)
        one = slice(g, g + 1)
        offset = (codes_ref[:, span] - zp_ref[:, one]).astype(F32)
        vals[isl, :, span] = (step_ref[:, one] * offset + min_ref[:, one]).astype(BF16)
    for hop in range(1, islands):
        send(lambda hop=hop: (vals.at[isl], vals.at[isl], val_s.at[hop - 1], val_r.at[isl]),
             {"island": (isl + hop) % islands})

    acc[...] = jnp.zeros_like(acc)

    def use(zo, xo, first, count):
        def body(i, carry):
            r = pl.multiple_of(first + i * 128, 128)
            cols = pl.ds(pl.multiple_of((zo * 2 + xo) * rows + r, 128), 128)
            block = wf[zo, xo, pl.ds(r, 128), :]
            acc[...] += jnp.dot(tok[:, cols], block, preferred_element_type=F32)
            tg_ref[:, cols] = lax.dot_general(
                cot_ref[...], block, (((1,), (1,)), ((), ())), preferred_element_type=F32
            ).astype(BF16)
            return carry

        lax.fori_loop(0, count // 128, body, 0)

    def use_a(zo, xo):
        use(zo, xo, 0, rows_a)

    def use_b(zo, xo):
        use(zo, xo, rows_a, rows - rows_a)

    def add(write, reads, count):
        def body(i, carry):
            here = pl.ds(pl.multiple_of(i * 64, 64), 64)
            total = reads[0][here, :].astype(F32)
            for ref in reads[1:]:
                total += ref[here, :].astype(F32)
            write(here, total)
            return carry

        lax.fori_loop(0, count // 64, body, 0)

    def into(ref):
        def write(here, total):
            ref[here, :] = total.astype(BF16)
        return write

    gax_send(z, None)
    use(z, x, 0, rows)

    def gb_open():
        arrived(wf.at[z, ox, B], gbx.at[1])
        gb_send(z, x, True, True)
        gb_send(z, ox, True, True)

    rows_b = rows - rows_a

    for t in range(1, NZ):
        for zo, ok, up in ((z - t, z - t >= 0, True), (z + t, z + t < NZ, False)):
            @pl.when(ok)
            def _(zo=zo, ok=ok):
                arrived(wf.at[zo, x, A], ga_r.at[zo])
            if up:
                ga_send(zo, ok, False)
            else:
                ga_send(zo, False, ok)

            @pl.when(ok)
            def _(zo=zo, ok=ok):
                gax_send(zo, ok)

        zt = NZ - 1 - t + z
        c = jnp.logical_and(has_dn, zt < NZ)
        go = jnp.logical_and(c, zt > z)

        @pl.when(go)
        def _(zt=zt, go=go):
            for xo in range(2):
                arrived(up_b.at[zt, xo], sb_up.at[zt, xo])
                add(into(part.at[zt, xo, B]), [part.at[zt, xo, B], up_b.at[zt, xo]], rows_b)
                sb_send(zt, xo, True, go)

        zd = t + z - (NZ - 1)
        c = jnp.logical_and(has_up, zd >= 0)
        gd = jnp.logical_and(c, zd < z)

        @pl.when(gd)
        def _(zd=zd, gd=gd):
            for xo in range(2):
                arrived(dn_b.at[zd, xo], sb_dn.at[zd, xo])
                add(into(part.at[zd, xo, B]), [part.at[zd, xo, B], dn_b.at[zd, xo]], rows_b)
                sb_send(zd, xo, False, gd)

        if t == 1:
            gb_open()
            use_b(z, ox)
        for zo, ok in ((z - t, z - t >= 0), (z + t, z + t < NZ)):
            @pl.when(ok)
            def _(zo=zo):
                use_a(zo, x)

    def b_sums(xo, write):
        own = part.at[z, xo, B]

        @pl.when(has_dn)
        def _():
            arrived(up_b.at[z, xo], sb_up.at[z, xo])

        @pl.when(has_up)
        def _():
            arrived(dn_b.at[z, xo], sb_dn.at[z, xo])

        @pl.when(jnp.logical_and(has_dn, has_up))
        def _():
            add(write, [own, up_b.at[z, xo], dn_b.at[z, xo]], rows_b)

        @pl.when(jnp.logical_not(has_dn))
        def _():
            add(write, [own, dn_b.at[z, xo]], rows_b)

        @pl.when(jnp.logical_not(has_up))
        def _():
            add(write, [own, up_b.at[z, xo]], rows_b)

    def wg_b(here, total):
        wg_ref[pl.ds(pl.multiple_of(rows_a + here.start, 64), 64), :] = total

    def sa_send(zt, up, cond):
        if up:
            send(lambda: (part.at[zt, x, A], up_a.at[zt], sa_s.at[zt], sa_up.at[zt]), above, cond)
        else:
            send(lambda: (part.at[zt, x, A], dn_a.at[zt], sa_s.at[zt], sa_dn.at[zt]), below, cond)

    for zt in (NZ - 1, 0, 2, 1):
        arrived(xr_a.at[zt], sax_r.at[zt])
        edge = []
        if zt > 0:
            edge.append((z == 0, True))
        if zt < NZ - 1:
            edge.append((z == NZ - 1, False))
        for c, up in edge:
            @pl.when(c)
            def _(zt=zt, c=c, up=up):
                add(into(part.at[zt, x, A]), [part.at[zt, x, A], xr_a.at[zt]], rows_a)
                sa_send(zt, up, c)

    b_sums(ox, into(part.at[z, ox, B]))
    send(lambda: (part.at[z, ox, B], xr_b, sbx.at[0], sbx.at[1]), flip)
    b_sums(x, wg_b)

    arrived(wf.at[z, ox, A], gax_r.at[z])
    use_a(z, ox)

    for hop in range(1, islands):
        other = (isl + hop) % islands
        arrived(vals.at[other], val_r.at[other])

    width = codes_ref.shape[1]

    def outer(i, carry):
        span = pl.ds(pl.multiple_of(i * 512, 512), 512)
        total = vals[0, :, span].astype(F32)
        for j in range(1, islands):
            total += vals[j, :, span].astype(F32)
        delta = total / islands
        new = 0.9 * mom_ref[:, span] + delta
        nmom_ref[:, span] = new
        npar_ref[:, span] = par_ref[:, span] - 0.7 * (delta + 0.9 * new)
        return carry

    lax.fori_loop(0, width // 512, outer, 0)

    for t in range(1, NZ):
        zt = NZ - 1 - t + z
        go = jnp.logical_and(jnp.logical_and(has_dn, zt < NZ), zt > z)

        @pl.when(go)
        def _(zt=zt, go=go):
            arrived(up_a.at[zt], sa_up.at[zt])
            add(into(part.at[zt, x, A]), [part.at[zt, x, A], xr_a.at[zt], up_a.at[zt]], rows_a)
            sa_send(zt, True, go)

        zd = t + z - (NZ - 1)
        gd = jnp.logical_and(jnp.logical_and(has_up, zd >= 0), zd < z)

        @pl.when(gd)
        def _(zd=zd, gd=gd):
            arrived(dn_a.at[zd], sa_dn.at[zd])
            add(into(part.at[zd, x, A]), [part.at[zd, x, A], xr_a.at[zd], dn_a.at[zd]], rows_a)
            sa_send(zd, False, gd)

        for zo, ok, up in ((z - t, z - t >= 0, True), (z + t, z + t < NZ, False)):
            for xo in range(2):
                @pl.when(ok)
                def _(zo=zo, xo=xo):
                    arrived(wf.at[zo, xo, B], gb_r.at[zo, xo])
                if up:
                    gb_send(zo, xo, ok, False)
                else:
                    gb_send(zo, xo, False, ok)

        for zo, ok in ((z - t, z - t >= 0), (z + t, z + t < NZ)):
            @pl.when(ok)
            def _(zo=zo):
                use_b(zo, 0)
                use_b(zo, 1)
                arrived(wf.at[zo, ox, A], gax_r.at[zo])
                use_a(zo, ox)

    proj_ref[...] = acc[...].astype(BF16)

    arrived(xr_b, sbx.at[1])

    def last_b(i, carry):
        here = pl.ds(pl.multiple_of(i * 64, 64), 64)
        there = pl.ds(pl.multiple_of(rows_a + i * 64, 64), 64)
        wg_ref[there, :] = (wg_ref[there, :] + xr_b[here, :].astype(F32)) * scaling
        return carry

    lax.fori_loop(0, rows_b // 64, last_b, 0)

    def wg_a(here, total):
        wg_ref[here, :] = total * scaling

    own = [part.at[z, x, A], xr_a.at[z]]

    @pl.when(has_dn)
    def _():
        arrived(up_a.at[z], sa_up.at[z])

    @pl.when(has_up)
    def _():
        arrived(dn_a.at[z], sa_dn.at[z])

    @pl.when(jnp.logical_and(has_dn, has_up))
    def _():
        add(wg_a, own + [up_a.at[z], dn_a.at[z]], rows_a)

    @pl.when(jnp.logical_not(has_dn))
    def _():
        add(wg_a, own + [dn_a.at[z]], rows_a)

    @pl.when(jnp.logical_not(has_up))
    def _():
        add(wg_a, own + [up_a.at[z]], rows_a)

    for cond, copy in pending:
        if cond is None:
            copy().wait_send()
        else:
            pl.when(cond)(lambda copy=copy: copy().wait_send())


def grid_local(
    islands,
    tokens, cotangent, key_weight, quant_codes, zero_points, minima, quant_steps, momentum, params
):
    tok_rows, width = tokens.shape[1:]
    rows, heads = key_weight.shape[1:]
    frag = quant_codes.shape[1]
    rows_a = rows // 128 * 5 // 8 * 128
    rows_b = rows - rows_a
    scaling = 1.0 / math.sqrt(tok_rows * 2 * NZ)
    vmem = pl.BlockSpec(memory_space=pltpu.VMEM)
    hbm = pl.BlockSpec(memory_space=pl.ANY)
    dma = pltpu.SemaphoreType.DMA
    outs = pl.pallas_call(
        functools.partial(kernel, islands, rows_a, scaling),
        out_shape=(
            jax.ShapeDtypeStruct((tok_rows, heads), BF16),
            jax.ShapeDtypeStruct((tok_rows, width), BF16),
            jax.ShapeDtypeStruct((rows, heads), F32),
            jax.ShapeDtypeStruct((frag, width), F32),
            jax.ShapeDtypeStruct((frag, width), F32),
        ),
        in_specs=[hbm, vmem, hbm] + [vmem] * 6,
        out_specs=[vmem] * 5,
        scratch_shapes=[
            pltpu.VMEM((tok_rows, width), BF16),
            pltpu.VMEM((NZ, 2, rows, heads), BF16),
            pltpu.VMEM((NZ, 2, rows, heads), BF16),
            pltpu.VMEM((NZ, rows_a, heads), BF16),
            pltpu.VMEM((NZ, rows_a, heads), BF16),
            pltpu.VMEM((NZ, rows_a, heads), BF16),
            pltpu.VMEM((NZ, 2, rows_b, heads), BF16),
            pltpu.VMEM((NZ, 2, rows_b, heads), BF16),
            pltpu.VMEM((rows_b, heads), BF16),
            pltpu.VMEM((islands, frag, width), BF16),
            pltpu.VMEM((tok_rows, heads), F32),
            dma((2,)),
            dma((NZ,)), dma((NZ,)), dma((NZ,)), dma((NZ,)), dma((NZ,)), dma((2,)),
            dma((NZ, 2)), dma((NZ, 2)), dma((NZ, 2)),
            dma((NZ,)), dma((NZ,)), dma((NZ,)), dma((NZ,)), dma((NZ,)),
            dma((NZ, 2)), dma((NZ, 2)), dma((NZ, 2)), dma((2,)),
            dma((islands - 1,)), dma((islands,)),
        ],
        compiler_params=pltpu.CompilerParams(
            collective_id=0, has_side_effects=True, vmem_limit_bytes=60 * 2**20
        ),
        cost_estimate=pl.CostEstimate(
            flops=6 * tok_rows * width * heads, bytes_accessed=20 * 2**20, transcendentals=0
        ),
    )(
        tokens[0], cotangent[0], key_weight[0], quant_codes[0], zero_points[0], minima[0],
        quant_steps[0], momentum, params,
    )
    projected, token_grad, weight_grad, new_momentum, new_params = outs
    return (projected[None], token_grad[None], weight_grad[None], new_momentum, new_params)


def solution(mesh):
    placed = (P("island", "fsdp", None),) * 7 + (P("fsdp", None),) * 2
    if mesh.shape["fsdp"] == 2 * NZ:
        body = functools.partial(grid_local, mesh.shape["island"])
    else:
        body = local
    return jax.shard_map(
        body,
        mesh=mesh,
        in_specs=placed,
        out_specs=(P("island", "fsdp", None),) * 3 + (P("fsdp", None),) * 2,
        check_vma=False,
    )
```

time: 436 us -> 169 us (0.39)
  waiting for transfers between devices: 388 us -> 0 us
  Pallas kernels: 0 us -> 159 us
  matrix products: 21.3 us -> 0 us
  between operations: 15.5 us -> 0.65 us
  other arithmetic: 7.82 us -> 0 us
  local copies, waits for them, and re-layouts: 2.72 us -> 9.42 us
    reduce_scatter x1 -> x0, waiting for transfers between devices: 271 us -> none  [local(): lax.psum_scatter(lax.dot_general(columns, cot_rows, (((0,), (0,)), ((), (...]
    pallas_call x0 -> x1, Pallas kernels: none -> 159 us  [grid_local(): pl.pallas_call(functools.partial(kernel, islands, rows_a, scaling), out_s...]
    all_gather x1 -> x0, waiting for transfers between devices: 92.8 us -> none  [local(): piece = lax.all_gather(weight, 'fsdp', axis=0, tiled=True)]
    psum x1 -> x0, waiting for transfers between devices: 24 us -> none  [local(): summed = lax.psum(values.astype(jnp.bfloat16), 'island').astype(jnp.float32)]
    dot_general x3 -> x0, matrix products: 21.3 us -> none  [the longest x1 10.3 us: local(): lax.dot_general(columns, cot_rows, (((0,), (0,)), ((), ())), preferred_el...]
    unnamed x10 -> x11, local copies, waits for them, and re-layouts: 0.02 us -> 9.42 us
  transfers between devices with their start and end apart: 3 -> 0, of which waited for: 3 -> 0; matrix products, arithmetic and copies ran while one was open for 5% -> 0% of each run, Pallas kernels for 0% -> 0%
where the time goes in v1:
time: 169 us
  Pallas kernels  159 us (94%)
  local copies, waits for them, and re-layouts  9.42 us (6%)
    pallas_call x1, Pallas kernels, grid_local(): pl.pallas_call(functools.partial(kernel, islands, rows_a, scaling), out_s...  159 us
    unnamed x11, local copies, waits for them, and re-layouts  9.42 us

profile of v1, /device:TPU:0, one launch (start us, length us, event | category | flops | bytes accessed | tf_op | source)
XLA Modules:
  0.0 169.2 jit_solution(10472271124588387272)
XLA Ops:
  0.6 159.2 %shard_map.128 = (bf16[256,512]{1,0:T(8,128)(2,1)}, bf16[256,8192]{1,0:T(8,128)(2,1)}, f32[1024,512]{1,0:T(8,128)}, f32[16,8192]{1,0:T(8,128)}, f32[16,8192]{1,0:T(8,128)}) custom-call(bf16[256,8192]{1,0:T(8,128)(2,1)} %bitcast.13, bf16[256,512]{1,0:T(8,128)(2,1)} %bitcast.16, bf16[1024,512]{1,0:T(8,128)(2,1)} %bitcast.14, s32[16,8192]{1,0:T(8,128)} %bitcast.15, ...), custom_call_target="tpu_custom_call" | custom-call | flops 6442450944 | bytes 20971520 | tf_op jit(solution)/shard_map/pallas_call | solution.py:450
  159.8 1.7 copy.19
  161.5 0.0 copy-start
  161.5 4.8 %copy.20 = bf16[1,256,8192]{2,1,0:T(8,128)(2,1)} copy(bf16[1,256,8192]{2,1,0:T(8,128)(2,1)} %bitcast.10) | data formatting | bytes 8388608
  166.3 0.0 copy-done
  166.3 0.0 copy-start.2
  166.3 0.0 copy-start.1
  166.3 1.3 copy.21
  167.6 0.1 copy-done.2
  167.6 0.8 copy.22
  168.4 0.0 copy-done.1
  168.4 0.8 copy.23
Async XLA Ops:
  161.5 4.8 %copy-start = (f32[1024,512]{1,0:T(8,128)S(1)}, f32[1024,512]{1,0:T(8,128)}, u32[]{:S(2)}) copy-start(f32[1024,512]{1,0:T(8,128)} %get-tuple-element.12) | copy-start | bytes 6291460
  166.3 1.4 copy-start.2
  166.3 2.2 %copy-start.1 = (f32[16,8192]{1,0:T(8,128)S(1)}, f32[16,8192]{1,0:T(8,128)}, u32[]{:S(2)}) copy-start(f32[16,8192]{1,0:T(8,128)} %get-tuple-element.24) | copy-start | bytes 1572868

commit v2 on v1

--- a/solution.py
+++ b/solution.py
@@ -75,13 +75,14 @@
 
     pending = []
 
-    def send(make, to, cond=None):
+    def send(make, to, cond=None, early=None):
         def copy():
             src, dst, ssem, rsem = make()
             return pltpu.make_async_remote_copy(
                 src_ref=src, dst_ref=dst, send_sem=ssem, recv_sem=rsem,
                 device_id=to, device_id_type=MESH)
-        pending.append((cond, copy))
+        if early is not True:
+            pending.append((cond, early, copy))
         copy().start()
 
     def arrived(dst, rsem):
@@ -110,49 +111,79 @@
             barrier, inc=1, device_id={"island": (isl + hop) % islands}, device_id_type=MESH)
     pl.semaphore_wait(barrier, islands + has_up.astype(jnp.int32) + has_dn.astype(jnp.int32))
 
-    def ga_send(zo, up, dn):
+    first, last = z == 0, z == NZ - 1
+
+    def ga_send(zo, up, dn, own=False):
         c_up = jnp.logical_and(has_up, up)
         c_dn = jnp.logical_and(has_dn, dn)
 
         @pl.when(c_up)
         def _():
-            send(lambda: (wf.at[zo, x, A], wf.at[zo, x, A], ga_up.at[zo], ga_r.at[zo]), above, c_up)
+            send(lambda: (wf.at[zo, x, A], wf.at[zo, x, A], ga_up.at[zo], ga_r.at[zo]), above, c_up,
+                 first if own else None)
 
         @pl.when(c_dn)
         def _():
-            send(lambda: (wf.at[zo, x, A], wf.at[zo, x, A], ga_dn.at[zo], ga_r.at[zo]), below, c_dn)
+            send(lambda: (wf.at[zo, x, A], wf.at[zo, x, A], ga_dn.at[zo], ga_r.at[zo]), below, c_dn,
+                 last if own else None)
 
     def gax_send(zo, cond):
         send(lambda: (wf.at[zo, x, A], wf.at[zo, x, A], gax_s.at[zo], gax_r.at[zo]), flip, cond)
 
-    def gb_send(zo, xo, up, dn):
+    def gb_send(zo, xo, up, dn, own=False):
         c_up = jnp.logical_and(has_up, up)
         c_dn = jnp.logical_and(has_dn, dn)
 
         @pl.when(c_up)
         def _():
             send(lambda: (wf.at[zo, xo, B], wf.at[zo, xo, B], gb_up.at[zo, xo], gb_r.at[zo, xo]),
-                 above, c_up)
+                 above, c_up, first if own else None)
 
         @pl.when(c_dn)
         def _():
             send(lambda: (wf.at[zo, xo, B], wf.at[zo, xo, B], gb_dn.at[zo, xo], gb_r.at[zo, xo]),
-                 below, c_dn)
+                 below, c_dn, last if own else None)
 
     w_in.wait()
     send(lambda: (wf.at[z, x, B], wf.at[z, x, B], gbx.at[0], gbx.at[1]), flip)
-    ga_send(z, True, True)
+    ga_send(z, True, True, own=True)
 
     tok_in.wait()
     cot = cot_ref[...]
 
-    def sb_send(zt, xo, up, cond):
+    def sb_send(zt, xo, up, cond, early=None):
         if up:
             send(lambda: (part.at[zt, xo, B], up_b.at[zt, xo], sb_s.at[zt, xo], sb_up.at[zt, xo]),
-                 above, cond)
+                 above, cond, early)
         else:
             send(lambda: (part.at[zt, xo, B], dn_b.at[zt, xo], sb_s.at[zt, xo], sb_dn.at[zt, xo]),
-                 below, cond)
+                 below, cond, early)
+
+    def sent(make, to):
+        src, dst, ssem, rsem = make()
+        pltpu.make_async_remote_copy(
+            src_ref=src, dst_ref=dst, send_sem=ssem, recv_sem=rsem,
+            device_id=to, device_id_type=MESH).wait_send()
+
+    def sb_start(t, up):
+        end = 0 if up else NZ - 1
+        zt = NZ - 1 - t if up else t
+        c = z == end
+        to = above if up else below
+
+        @pl.when(c)
+        def _():
+            if t == 0:
+                if up:
+                    sent(lambda: (wf.at[z, x, A], wf.at[z, x, A], ga_up.at[z], ga_r.at[z]), to)
+                else:
+                    sent(lambda: (wf.at[z, x, A], wf.at[z, x, A], ga_dn.at[z], ga_r.at[z]), to)
+            else:
+                before = zt + 1 if up else zt - 1
+                sent(lambda: (part.at[before, 0, B], up_b.at[before, 0], sb_s.at[before, 0],
+                              sb_up.at[before, 0]), to)
+            for xo in range(2):
+                sb_send(zt, xo, up, c, True if xo == 0 and t < NZ - 2 else None)
 
     tile = 256
     tiles = rows // tile
@@ -167,20 +198,6 @@
 
         lax.fori_loop(0, 2 * tiles, grad_tile, 0)
         send(lambda zt=zt: (part.at[zt, ox, A], xr_a.at[zt], sax_s.at[zt], sax_r.at[zt]), flip)
-        if zt > 0:
-            c0 = z == 0
-
-            @pl.when(c0)
-            def _(zt=zt):
-                for xo in range(2):
-                    sb_send(zt, xo, True, c0)
-        if zt < NZ - 1:
-            c3 = z == NZ - 1
-
-            @pl.when(c3)
-            def _(zt=zt):
-                for xo in range(2):
-                    sb_send(zt, xo, False, c3)
 
     for g in range(zp_ref.shape[1]):
         span = slice(g * GROUP, (g + 1) * GROUP)
@@ -229,11 +246,13 @@
         return write
 
     gax_send(z, None)
+    sb_start(0, True)
+    sb_start(0, False)
     use(z, x, 0, rows)
 
     def gb_open():
         arrived(wf.at[z, ox, B], gbx.at[1])
-        gb_send(z, x, True, True)
+        gb_send(z, x, True, True, own=True)
         gb_send(z, ox, True, True)
 
     rows_b = rows - rows_a
@@ -274,9 +293,11 @@
                 add(into(part.at[zd, xo, B]), [part.at[zd, xo, B], dn_b.at[zd, xo]], rows_b)
                 sb_send(zd, xo, False, gd)
 
-        if t == 1:
+        if t < NZ - 1:
+            sb_start(t, True)
+            sb_start(t, False)
+        if t == NZ - 2:
             gb_open()
-            use_b(z, ox)
         for zo, ok in ((z - t, z - t >= 0), (z + t, z + t < NZ)):
             @pl.when(ok)
             def _(zo=zo):
@@ -308,24 +329,38 @@
     def wg_b(here, total):
         wg_ref[pl.ds(pl.multiple_of(rows_a + here.start, 64), 64), :] = total
 
-    def sa_send(zt, up, cond):
+    def sa_send(zt, up, cond, early=None):
         if up:
-            send(lambda: (part.at[zt, x, A], up_a.at[zt], sa_s.at[zt], sa_up.at[zt]), above, cond)
+            send(lambda: (part.at[zt, x, A], up_a.at[zt], sa_s.at[zt], sa_up.at[zt]), above, cond,
+                 early)
         else:
-            send(lambda: (part.at[zt, x, A], dn_a.at[zt], sa_s.at[zt], sa_dn.at[zt]), below, cond)
+            send(lambda: (part.at[zt, x, A], dn_a.at[zt], sa_s.at[zt], sa_dn.at[zt]), below, cond,
+                 early)
+
+    def sa_start(t, up):
+        zt = NZ - 1 - t if up else t
+        c = first if up else last
+        to = above if up else below
+
+        @pl.when(c)
+        def _():
+            add(into(part.at[zt, x, A]), [part.at[zt, x, A], xr_a.at[zt]], rows_a)
+            if t == 0:
+                if up:
+                    sent(lambda: (wf.at[z, x, B], wf.at[z, x, B], gb_up.at[z, x], gb_r.at[z, x]), to)
+                else:
+                    sent(lambda: (wf.at[z, x, B], wf.at[z, x, B], gb_dn.at[z, x], gb_r.at[z, x]), to)
+            else:
+                before = zt + 1 if up else zt - 1
+                sent(lambda: (part.at[before, x, A], up_a.at[before], sa_s.at[before],
+                              sa_up.at[before]), to)
+            sa_send(zt, up, c, True if t < NZ - 2 else None)
 
     for zt in (NZ - 1, 0, 2, 1):
         arrived(xr_a.at[zt], sax_r.at[zt])
-        edge = []
-        if zt > 0:
-            edge.append((z == 0, True))
-        if zt < NZ - 1:
-            edge.append((z == NZ - 1, False))
-        for c, up in edge:
-            @pl.when(c)
-            def _(zt=zt, c=c, up=up):
-                add(into(part.at[zt, x, A]), [part.at[zt, x, A], xr_a.at[zt]], rows_a)
-                sa_send(zt, up, c)
+    use_b(z, ox)
+    sa_start(0, True)
+    sa_start(0, False)
 
     b_sums(ox, into(part.at[z, ox, B]))
     send(lambda: (part.at[z, ox, B], xr_b, sbx.at[0], sbx.at[1]), flip)
@@ -354,24 +389,6 @@
     lax.fori_loop(0, width // 512, outer, 0)
 
     for t in range(1, NZ):
-        zt = NZ - 1 - t + z
-        go = jnp.logical_and(jnp.logical_and(has_dn, zt < NZ), zt > z)
-
-        @pl.when(go)
-        def _(zt=zt, go=go):
-            arrived(up_a.at[zt], sa_up.at[zt])
-            add(into(part.at[zt, x, A]), [part.at[zt, x, A], xr_a.at[zt], up_a.at[zt]], rows_a)
-            sa_send(zt, True, go)
-
-        zd = t + z - (NZ - 1)
-        gd = jnp.logical_and(jnp.logical_and(has_up, zd >= 0), zd < z)
-
-        @pl.when(gd)
-        def _(zd=zd, gd=gd):
-            arrived(dn_a.at[zd], sa_dn.at[zd])
-            add(into(part.at[zd, x, A]), [part.at[zd, x, A], xr_a.at[zd], dn_a.at[zd]], rows_a)
-            sa_send(zd, False, gd)
-
         for zo, ok, up in ((z - t, z - t >= 0, True), (z + t, z + t < NZ, False)):
             for xo in range(2):
                 @pl.when(ok)
@@ -382,6 +399,28 @@
                 else:
                     gb_send(zo, xo, False, ok)
 
+        zt = NZ - 1 - t + z
+        go = jnp.logical_and(jnp.logical_and(has_dn, zt < NZ), zt > z)
+
+        @pl.when(go)
+        def _(zt=zt, go=go):
+            arrived(up_a.at[zt], sa_up.at[zt])
+            add(into(part.at[zt, x, A]), [part.at[zt, x, A], xr_a.at[zt], up_a.at[zt]], rows_a)
+            sa_send(zt, True, go)
+
+        zd = t + z - (NZ - 1)
+        gd = jnp.logical_and(jnp.logical_and(has_up, zd >= 0), zd < z)
+
+        @pl.when(gd)
+        def _(zd=zd, gd=gd):
+            arrived(dn_a.at[zd], sa_dn.at[zd])
+            add(into(part.at[zd, x, A]), [part.at[zd, x, A], xr_a.at[zd], dn_a.at[zd]], rows_a)
+            sa_send(zd, False, gd)
+
+        if t < NZ - 1:
+            sa_start(t, True)
+            sa_start(t, False)
+
         for zo, ok in ((z - t, z - t >= 0), (z + t, z + t < NZ)):
             @pl.when(ok)
             def _(zo=zo):
@@ -427,7 +466,9 @@
     def _():
         add(wg_a, own + [up_a.at[z]], rows_a)
 
-    for cond, copy in pending:
+    for cond, early, copy in pending:
+        if early is not None:
+            cond = jnp.logical_and(cond, jnp.logical_not(early))
         if cond is None:
             copy().wait_send()
         else:

time: 169 us -> 163 us (0.964)
  Pallas kernels: 159 us -> 152 us
    pallas_call x1, Pallas kernels: 159 us -> 152 us  [grid_local(): pl.pallas_call(functools.partial(kernel, islands, rows_a, scaling), out_s...]
where the time goes in v2:
time: 163 us; the launch traced here: 162 us
  Pallas kernels  152 us (93%)
  local copies, waits for them, and re-layouts  9.42 us (6%)
    pallas_call x1, Pallas kernels, grid_local(): pl.pallas_call(functools.partial(kernel, islands, rows_a, scaling), out_s...  152 us
    unnamed x11, local copies, waits for them, and re-layouts  9.42 us

profile of v2, /device:TPU:0, one launch (start us, length us, event | category | flops | bytes accessed | tf_op | source)
XLA Modules:
  0.0 162.5 jit_solution(7931338143578138573)
XLA Ops:
  0.6 152.4 %shard_map.128 = (bf16[256,512]{1,0:T(8,128)(2,1)}, bf16[256,8192]{1,0:T(8,128)(2,1)}, f32[1024,512]{1,0:T(8,128)}, f32[16,8192]{1,0:T(8,128)}, f32[16,8192]{1,0:T(8,128)}) custom-call(bf16[256,8192]{1,0:T(8,128)(2,1)} %bitcast.13, bf16[256,512]{1,0:T(8,128)(2,1)} %bitcast.16, bf16[1024,512]{1,0:T(8,128)(2,1)} %bitcast.14, s32[16,8192]{1,0:T(8,128)} %bitcast.15, ...), custom_call_target="tpu_custom_call" | custom-call | flops 6442450944 | bytes 20971520 | tf_op jit(solution)/shard_map/pallas_call | solution.py:491
  153.0 1.7 %copy.19 = bf16[1,256,512]{2,1,0:T(8,128)(2,1)} copy(bf16[1,256,512]{2,1,0:T(8,128)(2,1)} %bitcast.12) | data formatting | bytes 524288
  154.7 0.0 copy-start
  154.7 4.8 %copy.20 = bf16[1,256,8192]{2,1,0:T(8,128)(2,1)} copy(bf16[1,256,8192]{2,1,0:T(8,128)(2,1)} %bitcast.10) | data formatting | bytes 8388608
  159.5 0.0 copy-done
  159.5 0.0 copy-start.2
  159.5 0.0 copy-start.1
  159.5 1.3 copy.21
  160.8 0.1 copy-done.2
  160.9 0.8 copy.22
  161.7 0.0 copy-done.1
  161.7 0.8 copy.23
Async XLA Ops:
  154.7 4.8 %copy-start = (f32[1024,512]{1,0:T(8,128)S(1)}, f32[1024,512]{1,0:T(8,128)}, u32[]{:S(2)}) copy-start(f32[1024,512]{1,0:T(8,128)} %get-tuple-element.12) | copy-start | bytes 6291460
  159.5 1.4 copy-start.2
  159.5 2.2 %copy-start.1 = (f32[16,8192]{1,0:T(8,128)S(1)}, f32[16,8192]{1,0:T(8,128)}, u32[]{:S(2)}) copy-start(f32[16,8192]{1,0:T(8,128)} %get-tuple-element.24) | copy-start | bytes 1572868

commit v3 on v2

--- a/solution.py
+++ b/solution.py
@@ -54,9 +54,9 @@
 
 def kernel(
     islands, rows_a, scaling,
-    tok_hbm, cot_ref, w_hbm, codes_ref, zp_ref, min_ref, step_ref, mom_ref, par_ref,
+    tok_hbm, cot_hbm, w_hbm, codes_hbm, zp_hbm, min_hbm, step_hbm, mom_hbm, par_hbm,
     proj_ref, tg_ref, wg_ref, nmom_ref, npar_ref,
-    tok, wf, part, xr_a, up_a, dn_a, up_b, dn_b, xr_b, vals, acc,
+    tok, cot_ref, codes_ref, zp_ref, min_ref, step_ref, mom_ref, par_ref, wf, part, xr_a, up_a, dn_a, up_b, dn_b, xr_b, vals, acc,
     in_sem, ga_up, ga_dn, ga_r, gax_s, gax_r, gbx, gb_up, gb_dn, gb_r,
     sax_s, sax_r, sa_s, sa_up, sa_dn, sb_s, sb_up, sb_dn, sbx, val_s, val_r,
 ):
@@ -92,8 +92,18 @@
 
     tok_in = pltpu.make_async_copy(tok_hbm, tok, in_sem.at[0])
     w_in = pltpu.make_async_copy(w_hbm, wf.at[z, x], in_sem.at[1])
+    cot_in = pltpu.make_async_copy(cot_hbm, cot_ref, in_sem.at[2])
+    quant_in = [
+        pltpu.make_async_copy(src, dst, in_sem.at[3 + i])
+        for i, (src, dst) in enumerate((
+            (codes_hbm, codes_ref), (zp_hbm, zp_ref), (min_hbm, min_ref), (step_hbm, step_ref),
+            (mom_hbm, mom_ref), (par_hbm, par_ref)))
+    ]
     w_in.start()
+    cot_in.start()
     tok_in.start()
+    for copy in quant_in:
+        copy.start()
 
     barrier = pltpu.get_barrier_semaphore()
     pl.semaphore_signal(barrier, inc=1, device_id=flip, device_id_type=MESH)
@@ -148,6 +158,7 @@
     send(lambda: (wf.at[z, x, B], wf.at[z, x, B], gbx.at[0], gbx.at[1]), flip)
     ga_send(z, True, True, own=True)
 
+    cot_in.wait()
     tok_in.wait()
     cot = cot_ref[...]
 
@@ -199,6 +210,9 @@
         lax.fori_loop(0, 2 * tiles, grad_tile, 0)
         send(lambda zt=zt: (part.at[zt, ox, A], xr_a.at[zt], sax_s.at[zt], sax_r.at[zt]), flip)
 
+    for copy in quant_in:
+        copy.wait()
+
     for g in range(zp_ref.shape[1]):
         span = slice(g * GROUP, (g + 1) * GROUP)
         one = slice(g, g + 1)
@@ -245,7 +259,6 @@
             ref[here, :] = total.astype(BF16)
         return write
 
-    gax_send(z, None)
     sb_start(0, True)
     sb_start(0, False)
     use(z, x, 0, rows)
@@ -267,10 +280,6 @@
             else:
                 ga_send(zo, False, ok)
 
-            @pl.when(ok)
-            def _(zo=zo, ok=ok):
-                gax_send(zo, ok)
-
         zt = NZ - 1 - t + z
         c = jnp.logical_and(has_dn, zt < NZ)
         go = jnp.logical_and(c, zt > z)
@@ -298,6 +307,8 @@
             sb_start(t, False)
         if t == NZ - 2:
             gb_open()
+            arrived(xr_a.at[NZ - 1], sax_r.at[NZ - 1])
+            gax_send(z, None)
         for zo, ok in ((z - t, z - t >= 0), (z + t, z + t < NZ)):
             @pl.when(ok)
             def _(zo=zo):
@@ -356,8 +367,12 @@
                               sa_up.at[before]), to)
             sa_send(zt, up, c, True if t < NZ - 2 else None)
 
-    for zt in (NZ - 1, 0, 2, 1):
+    for zt, t in ((0, 1), (2, 2), (1, 3)):
         arrived(xr_a.at[zt], sax_r.at[zt])
+        for zo, ok in ((z - t, z - t >= 0), (z + t, z + t < NZ)):
+            @pl.when(ok)
+            def _(zo=zo, ok=ok):
+                gax_send(zo, ok)
     use_b(z, ox)
     sa_start(0, True)
     sa_start(0, False)
@@ -481,26 +496,33 @@
 ):
     tok_rows, width = tokens.shape[1:]
     rows, heads = key_weight.shape[1:]
-    frag = quant_codes.shape[1]
+    frag, groups = zero_points.shape[1:]
     rows_a = rows // 128 * 5 // 8 * 128
     rows_b = rows - rows_a
     scaling = 1.0 / math.sqrt(tok_rows * 2 * NZ)
     vmem = pl.BlockSpec(memory_space=pltpu.VMEM)
-    hbm = pl.BlockSpec(memory_space=pl.ANY)
+    hbm = pl.BlockSpec(memory_space=pltpu.HBM)
     dma = pltpu.SemaphoreType.DMA
     outs = pl.pallas_call(
         functools.partial(kernel, islands, rows_a, scaling),
         out_shape=(
-            jax.ShapeDtypeStruct((tok_rows, heads), BF16),
-            jax.ShapeDtypeStruct((tok_rows, width), BF16),
-            jax.ShapeDtypeStruct((rows, heads), F32),
-            jax.ShapeDtypeStruct((frag, width), F32),
-            jax.ShapeDtypeStruct((frag, width), F32),
+            pltpu.VMEM((tok_rows, heads), BF16),
+            pltpu.VMEM((tok_rows, width), BF16),
+            pltpu.VMEM((rows, heads), F32),
+            pltpu.VMEM((frag, width), F32),
+            pltpu.VMEM((frag, width), F32),
         ),
-        in_specs=[hbm, vmem, hbm] + [vmem] * 6,
+        in_specs=[hbm] * 9,
         out_specs=[vmem] * 5,
         scratch_shapes=[
             pltpu.VMEM((tok_rows, width), BF16),
+            pltpu.VMEM((tok_rows, heads), BF16),
+            pltpu.VMEM((frag, width), jnp.int32),
+            pltpu.VMEM((frag, groups), jnp.int32),
+            pltpu.VMEM((frag, groups), F32),
+            pltpu.VMEM((frag, groups), F32),
+            pltpu.VMEM((frag, width), F32),
+            pltpu.VMEM((frag, width), F32),
             pltpu.VMEM((NZ, 2, rows, heads), BF16),
             pltpu.VMEM((NZ, 2, rows, heads), BF16),
             pltpu.VMEM((NZ, rows_a, heads), BF16),
@@ -511,7 +533,7 @@
             pltpu.VMEM((rows_b, heads), BF16),
             pltpu.VMEM((islands, frag, width), BF16),
             pltpu.VMEM((tok_rows, heads), F32),
-            dma((2,)),
+            dma((9,)),
             dma((NZ,)), dma((NZ,)), dma((NZ,)), dma((NZ,)), dma((NZ,)), dma((2,)),
             dma((NZ, 2)), dma((NZ, 2)), dma((NZ, 2)),
             dma((NZ,)), dma((NZ,)), dma((NZ,)), dma((NZ,)), dma((NZ,)),
@@ -519,7 +541,7 @@
             dma((islands - 1,)), dma((islands,)),
         ],
         compiler_params=pltpu.CompilerParams(
-            collective_id=0, has_side_effects=True, vmem_limit_bytes=60 * 2**20
+            collective_id=0, has_side_effects=True, vmem_limit_bytes=54 * 2**20
         ),
         cost_estimate=pl.CostEstimate(
             flops=6 * tok_rows * width * heads, bytes_accessed=20 * 2**20, transcendentals=0

time: 163 us -> 154 us (0.945)
  Pallas kernels: 152 us -> 148 us
  local copies, waits for them, and re-layouts: 9.42 us -> 5.62 us
    pallas_call x1, Pallas kernels: 152 us -> 148 us  [grid_local(): pl.pallas_call(functools.partial(kernel, islands, rows_a, scaling), out_s...]
    unnamed x11 -> x5, local copies, waits for them, and re-layouts: 9.42 us -> 5.62 us
where the time goes in v3:
time: 154 us
  Pallas kernels  148 us (96%)
  local copies, waits for them, and re-layouts  5.62 us (4%)
    pallas_call x1, Pallas kernels, grid_local(): pl.pallas_call(functools.partial(kernel, islands, rows_a, scaling), out_s...  148 us
    unnamed x5, local copies, waits for them, and re-layouts  5.62 us

profile of v3, /device:TPU:0, one launch (start us, length us, event | category | flops | bytes accessed | tf_op | source)
XLA Modules:
  0.0 154.3 jit_solution(989578010148767601)
XLA Ops:
  0.6 148.1 %shard_map.128 = (bf16[256,512]{1,0:T(8,128)(2,1)S(1)}, bf16[256,8192]{1,0:T(8,128)(2,1)S(1)}, f32[1024,512]{1,0:T(8,128)S(1)}, f32[16,8192]{1,0:T(8,128)S(1)}, f32[16,8192]{1,0:T(8,128)S(1)}) custom-call(bf16[256,8192]{1,0:T(8,128)(2,1)} %bitcast.13, bf16[256,512]{1,0:T(8,128)(2,1)} %bitcast.16, bf16[1024,512]{1,0:T(8,128)(2,1)} %bitcast.14, ...), custom_call_target="tpu_custom_call" | custom-call | flops 6442450944 | bytes 20971520 | tf_op jit(solution)/shard_map/pallas_call | solution.py:506
  148.7 0.7 copy.19
  149.4 2.0 %copy.20 = bf16[1,256,8192]{2,1,0:T(8,128)(2,1)} copy(bf16[1,256,8192]{2,1,0:T(8,128)(2,1)S(1)} %bitcast.10) | data formatting | bytes 8388608
  151.4 0.8 copy.22
  152.2 0.8 copy.23
  153.0 1.3 copy.21

commit v4 on v3

--- a/solution.py
+++ b/solution.py
@@ -237,22 +237,24 @@
 
         lax.fori_loop(0, count // 128, body, 0)
 
+    half = rows // 2
+
     def use_a(zo, xo):
-        use(zo, xo, 0, rows_a)
+        use(zo, xo, 0, half)
 
     def use_b(zo, xo):
-        use(zo, xo, rows_a, rows - rows_a)
+        use(zo, xo, half, rows - half)
 
     def add(write, reads, count):
         def body(i, carry):
-            here = pl.ds(pl.multiple_of(i * 64, 64), 64)
+            here = pl.ds(pl.multiple_of(i * 32, 32), 32)
             total = reads[0][here, :].astype(F32)
             for ref in reads[1:]:
                 total += ref[here, :].astype(F32)
             write(here, total)
             return carry
 
-        lax.fori_loop(0, count // 64, body, 0)
+        lax.fori_loop(0, count // 32, body, 0)
 
     def into(ref):
         def write(here, total):
@@ -338,7 +340,7 @@
             add(write, [own, up_b.at[z, xo]], rows_b)
 
     def wg_b(here, total):
-        wg_ref[pl.ds(pl.multiple_of(rows_a + here.start, 64), 64), :] = total
+        wg_ref[pl.ds(pl.multiple_of(rows_a + here.start, 32), 32), :] = total
 
     def sa_send(zt, up, cond, early=None):
         if up:
@@ -373,7 +375,6 @@
             @pl.when(ok)
             def _(zo=zo, ok=ok):
                 gax_send(zo, ok)
-    use_b(z, ox)
     sa_start(0, True)
     sa_start(0, False)
 
@@ -382,7 +383,7 @@
     b_sums(x, wg_b)
 
     arrived(wf.at[z, ox, A], gax_r.at[z])
-    use_a(z, ox)
+    use(z, ox, 0, rows)
 
     for hop in range(1, islands):
         other = (isl + hop) % islands
@@ -439,22 +440,21 @@
         for zo, ok in ((z - t, z - t >= 0), (z + t, z + t < NZ)):
             @pl.when(ok)
             def _(zo=zo):
-                use_b(zo, 0)
-                use_b(zo, 1)
+                use_b(zo, x)
                 arrived(wf.at[zo, ox, A], gax_r.at[zo])
-                use_a(zo, ox)
+                use(zo, ox, 0, rows)
 
     proj_ref[...] = acc[...].astype(BF16)
 
     arrived(xr_b, sbx.at[1])
 
     def last_b(i, carry):
-        here = pl.ds(pl.multiple_of(i * 64, 64), 64)
-        there = pl.ds(pl.multiple_of(rows_a + i * 64, 64), 64)
+        here = pl.ds(pl.multiple_of(i * 32, 32), 32)
+        there = pl.ds(pl.multiple_of(rows_a + i * 32, 32), 32)
         wg_ref[there, :] = (wg_ref[there, :] + xr_b[here, :].astype(F32)) * scaling
         return carry
 
-    lax.fori_loop(0, rows_b // 64, last_b, 0)
+    lax.fori_loop(0, rows_b // 32, last_b, 0)
 
     def wg_a(here, total):
         wg_ref[here, :] = total * scaling
@@ -490,6 +490,15 @@
             pl.when(cond)(lambda copy=copy: copy().wait_send())
 
 
+def write_out(*refs):
+    n = len(refs) // 2
+    copies = [pltpu.make_async_copy(refs[i], refs[n + i], refs[-1].at[i]) for i in range(n)]
+    for copy in copies:
+        copy.start()
+    for copy in copies:
+        copy.wait()
+
+
 def grid_local(
     islands,
     tokens, cotangent, key_weight, quant_codes, zero_points, minima, quant_steps, momentum, params
@@ -497,7 +506,7 @@
     tok_rows, width = tokens.shape[1:]
     rows, heads = key_weight.shape[1:]
     frag, groups = zero_points.shape[1:]
-    rows_a = rows // 128 * 5 // 8 * 128
+    rows_a = rows * 3 // 5 // 32 * 32
     rows_b = rows - rows_a
     scaling = 1.0 / math.sqrt(tok_rows * 2 * NZ)
     vmem = pl.BlockSpec(memory_space=pltpu.VMEM)
@@ -550,7 +559,14 @@
         tokens[0], cotangent[0], key_weight[0], quant_codes[0], zero_points[0], minima[0],
         quant_steps[0], momentum, params,
     )
-    projected, token_grad, weight_grad, new_momentum, new_params = outs
+    projected, token_grad, weight_grad, new_momentum, new_params = pl.pallas_call(
+        write_out,
+        out_shape=tuple(jax.ShapeDtypeStruct(out.shape, out.dtype) for out in outs),
+        in_specs=[pl.BlockSpec(memory_space=pl.ANY)] * len(outs),
+        out_specs=[hbm] * len(outs),
+        scratch_shapes=[dma((len(outs),))],
+        cost_estimate=pl.CostEstimate(flops=0, bytes_accessed=8 * 2**20, transcendentals=0),
+    )(*outs)
     return (projected[None], token_grad[None], weight_grad[None], new_momentum, new_params)
 
 

time: 154 us -> 384 us (2.49)
  Pallas kernels: 148 us -> 377 us
    pallas_call x0 -> x1, Pallas kernels: none -> 231 us  [grid_local(): pl.pallas_call(write_out, out_shape=tuple((jax.ShapeDtypeStruct(out.shape...]
where the time goes in v4:
time: 384 us
  Pallas kernels  377 us (98%)
  local copies, waits for them, and re-layouts  5.57 us (1%)
    pallas_call x1, Pallas kernels, grid_local(): pl.pallas_call(write_out, out_shape=tuple((jax.ShapeDtypeStruct(out.shape...  231 us
    pallas_call x1, Pallas kernels, grid_local(): pl.pallas_call(functools.partial(kernel, islands, rows_a, scaling), out_s...  146 us

profile of v4, /device:TPU:0, one launch (start us, length us, event | category | flops | bytes accessed | tf_op | source)
XLA Modules:
  0.0 383.6 jit_solution(5918543036436056290)
XLA Ops:
  0.6 146.0 %shard_map.128 = (bf16[256,512]{1,0:T(8,128)(2,1)S(1)}, bf16[256,8192]{1,0:T(8,128)(2,1)S(1)}, f32[1024,512]{1,0:T(8,128)S(1)}, f32[16,8192]{1,0:T(8,128)S(1)}, f32[16,8192]{1,0:T(8,128)S(1)}) custom-call(bf16[256,8192]{1,0:T(8,128)(2,1)} %bitcast.10, bf16[256,512]{1,0:T(8,128)(2,1)} %bitcast.15, bf16[1024,512]{1,0:T(8,128)(2,1)} %bitcast.13, ...), custom_call_target="tpu_custom_call" | custom-call | flops 6442450944 | bytes 20971520 | tf_op jit(solution)/shard_map/pallas_call | solution.py:515
  146.6 0.0 copy-start
  146.6 1.9 copy-done
  148.6 0.0 copy-start.1
  148.6 1.3 copy-done.1
  149.9 0.0 copy-start.2
  149.9 0.8 copy-done.2
  150.7 0.0 copy-start.3
  150.7 0.8 copy-done.3
  151.5 0.0 copy-start.4
  151.5 0.7 copy-done.4
  152.2 231.4 %shard_map.129 = (bf16[256,512]{1,0:T(8,128)(2,1)}, bf16[256,8192]{1,0:T(8,128)(2,1)}, f32[1024,512]{1,0:T(8,128)}, f32[16,8192]{1,0:T(8,128)}, f32[16,8192]{1,0:T(8,128)}) custom-call(bf16[256,512]{1,0:T(8,128)(2,1)} %copy-done.4, bf16[256,8192]{1,0:T(8,128)(2,1)} %copy-done, f32[1024,512]{1,0:T(8,128)} %copy-done.1, f32[16,8192]{1,0:T(8,128)} %copy-done.2, ...), custom_call_target="tpu_custom_call" | custom-call | bytes 8388608 | tf_op jit(solution)/shard_map/pallas_call | solution.py:562
Async XLA Ops:
  146.6 1.9 copy-start
  148.6 1.3 copy-start.1
  149.9 0.8 copy-start.2
  150.7 0.8 copy-start.3
  151.5 0.7 copy-start.4

commit v5 on v4

--- a/solution.py
+++ b/solution.py
@@ -210,6 +210,20 @@
         lax.fori_loop(0, 2 * tiles, grad_tile, 0)
         send(lambda zt=zt: (part.at[zt, ox, A], xr_a.at[zt], sax_s.at[zt], sax_r.at[zt]), flip)
 
+    sb_start(0, True)
+    sb_start(0, False)
+
+    def gather_a(t):
+        for zo, ok, up in ((z - t, z - t >= 0, True), (z + t, z + t < NZ, False)):
+            @pl.when(ok)
+            def _(zo=zo):
+                arrived(wf.at[zo, x, A], ga_r.at[zo])
+            if up:
+                ga_send(zo, ok, False)
+            else:
+                ga_send(zo, False, ok)
+
+    gather_a(1)
     for copy in quant_in:
         copy.wait()
 
@@ -261,8 +275,6 @@
             ref[here, :] = total.astype(BF16)
         return write
 
-    sb_start(0, True)
-    sb_start(0, False)
     use(z, x, 0, rows)
 
     def gb_open():
@@ -272,16 +284,8 @@
 
     rows_b = rows - rows_a
 
-    for t in range(1, NZ):
-        for zo, ok, up in ((z - t, z - t >= 0, True), (z + t, z + t < NZ, False)):
-            @pl.when(ok)
-            def _(zo=zo, ok=ok):
-                arrived(wf.at[zo, x, A], ga_r.at[zo])
-            if up:
-                ga_send(zo, ok, False)
-            else:
-                ga_send(zo, False, ok)
-
+    gather_a(2)
+    for t in range(1, NZ - 1):
         zt = NZ - 1 - t + z
         c = jnp.logical_and(has_dn, zt < NZ)
         go = jnp.logical_and(c, zt > z)
@@ -304,9 +308,8 @@
                 add(into(part.at[zd, xo, B]), [part.at[zd, xo, B], dn_b.at[zd, xo]], rows_b)
                 sb_send(zd, xo, False, gd)
 
-        if t < NZ - 1:
-            sb_start(t, True)
-            sb_start(t, False)
+        sb_start(t, True)
+        sb_start(t, False)
         if t == NZ - 2:
             gb_open()
             arrived(xr_a.at[NZ - 1], sax_r.at[NZ - 1])
@@ -316,6 +319,8 @@
             def _(zo=zo):
                 use_a(zo, x)
 
+    gather_a(NZ - 1)
+
     def b_sums(xo, write):
         own = part.at[z, xo, B]
 
@@ -338,6 +343,11 @@
         @pl.when(jnp.logical_not(has_up))
         def _():
             add(write, [own, up_b.at[z, xo]], rows_b)
+
+    for zo, ok in ((z - NZ + 1, z - NZ + 1 >= 0), (z + NZ - 1, z + NZ - 1 < NZ)):
+        @pl.when(ok)
+        def _(zo=zo):
+            use_a(zo, x)
 
     def wg_b(here, total):
         wg_ref[pl.ds(pl.multiple_of(rows_a + here.start, 32), 32), :] = total
@@ -437,12 +447,17 @@
             sa_start(t, True)
             sa_start(t, False)
 
+        ready = {1: (), 2: (1, 2), 3: (3,)}[t]
         for zo, ok in ((z - t, z - t >= 0), (z + t, z + t < NZ)):
             @pl.when(ok)
             def _(zo=zo):
                 use_b(zo, x)
-                arrived(wf.at[zo, ox, A], gax_r.at[zo])
-                use(zo, ox, 0, rows)
+        for k in ready:
+            for zo, ok in ((z - k, z - k >= 0), (z + k, z + k < NZ)):
+                @pl.when(ok)
+                def _(zo=zo):
+                    arrived(wf.at[zo, ox, A], gax_r.at[zo])
+                    use(zo, ox, 0, rows)
 
     proj_ref[...] = acc[...].astype(BF16)
 
@@ -488,15 +503,6 @@
             copy().wait_send()
         else:
             pl.when(cond)(lambda copy=copy: copy().wait_send())
-
-
-def write_out(*refs):
-    n = len(refs) // 2
-    copies = [pltpu.make_async_copy(refs[i], refs[n + i], refs[-1].at[i]) for i in range(n)]
-    for copy in copies:
-        copy.start()
-    for copy in copies:
-        copy.wait()
 
 
 def grid_local(
@@ -559,14 +565,7 @@
         tokens[0], cotangent[0], key_weight[0], quant_codes[0], zero_points[0], minima[0],
         quant_steps[0], momentum, params,
     )
-    projected, token_grad, weight_grad, new_momentum, new_params = pl.pallas_call(
-        write_out,
-        out_shape=tuple(jax.ShapeDtypeStruct(out.shape, out.dtype) for out in outs),
-        in_specs=[pl.BlockSpec(memory_space=pl.ANY)] * len(outs),
-        out_specs=[hbm] * len(outs),
-        scratch_shapes=[dma((len(outs),))],
-        cost_estimate=pl.CostEstimate(flops=0, bytes_accessed=8 * 2**20, transcendentals=0),
-    )(*outs)
+    projected, token_grad, weight_grad, new_momentum, new_params = outs
     return (projected[None], token_grad[None], weight_grad[None], new_momentum, new_params)
 
 

time: 384 us -> 150 us (0.39)
  Pallas kernels: 377 us -> 144 us
    pallas_call x1 -> x0, Pallas kernels: 231 us -> none  [grid_local(): pl.pallas_call(write_out, out_shape=tuple((jax.ShapeDtypeStruct(out.shape...]
where the time goes in v5:
time: 150 us
  Pallas kernels  144 us (96%)
  local copies, waits for them, and re-layouts  5.62 us (4%)
    pallas_call x1, Pallas kernels, grid_local(): pl.pallas_call(functools.partial(kernel, islands, rows_a, scaling), out_s...  144 us
    unnamed x5, local copies, waits for them, and re-layouts  5.62 us

profile of v5, /device:TPU:0, one launch (start us, length us, event | category | flops | bytes accessed | tf_op | source)
XLA Modules:
  0.0 150.3 jit_solution(15219865632814277964)
XLA Ops:
  0.6 144.0 %shard_map.128 = (bf16[256,512]{1,0:T(8,128)(2,1)S(1)}, bf16[256,8192]{1,0:T(8,128)(2,1)S(1)}, f32[1024,512]{1,0:T(8,128)S(1)}, f32[16,8192]{1,0:T(8,128)S(1)}, f32[16,8192]{1,0:T(8,128)S(1)}) custom-call(bf16[256,8192]{1,0:T(8,128)(2,1)} %bitcast.13, bf16[256,512]{1,0:T(8,128)(2,1)} %bitcast.16, bf16[1024,512]{1,0:T(8,128)(2,1)} %bitcast.14, ...), custom_call_target="tpu_custom_call" | custom-call | flops 6442450944 | bytes 20971520 | tf_op jit(solution)/shard_map/pallas_call | solution.py:521
  144.6 0.7 copy.19
  145.3 2.0 %copy.20 = bf16[1,256,8192]{2,1,0:T(8,128)(2,1)} copy(bf16[1,256,8192]{2,1,0:T(8,128)(2,1)S(1)} %bitcast.10) | data formatting | bytes 8388608
  147.4 0.8 copy.22
  148.2 0.8 copy.23
  148.9 1.3 copy.21

commit v6 on v5

--- a/solution.py
+++ b/solution.py
@@ -279,12 +279,13 @@
 
     def gb_open():
         arrived(wf.at[z, ox, B], gbx.at[1])
-        gb_send(z, x, True, True, own=True)
+        gb_send(z, x, z != NZ - 2, z != 1, own=True)
         gb_send(z, ox, True, True)
 
     rows_b = rows - rows_a
 
     gather_a(2)
+    gb_send(z, x, z == NZ - 2, z == 1)
     for t in range(1, NZ - 1):
         zt = NZ - 1 - t + z
         c = jnp.logical_and(has_dn, zt < NZ)

time: 150 us -> 150 us (level)
  no operation moved by 1% of the time
where the time goes in v6:
time: 150 us
  Pallas kernels  144 us (96%)
  local copies, waits for them, and re-layouts  5.62 us (4%)
    pallas_call x1, Pallas kernels, grid_local(): pl.pallas_call(functools.partial(kernel, islands, rows_a, scaling), out_s...  144 us
    unnamed x5, local copies, waits for them, and re-layouts  5.62 us

profile of v6, /device:TPU:0, one launch (start us, length us, event | category | flops | bytes accessed | tf_op | source)
XLA Modules:
  0.0 149.9 jit_solution(3547153259073205872)
XLA Ops:
  0.6 143.7 %shard_map.128 = (bf16[256,512]{1,0:T(8,128)(2,1)S(1)}, bf16[256,8192]{1,0:T(8,128)(2,1)S(1)}, f32[1024,512]{1,0:T(8,128)S(1)}, f32[16,8192]{1,0:T(8,128)S(1)}, f32[16,8192]{1,0:T(8,128)S(1)}) custom-call(bf16[256,8192]{1,0:T(8,128)(2,1)} %bitcast.13, bf16[256,512]{1,0:T(8,128)(2,1)} %bitcast.16, bf16[1024,512]{1,0:T(8,128)(2,1)} %bitcast.14, ...), custom_call_target="tpu_custom_call" | custom-call | flops 6442450944 | bytes 20971520 | tf_op jit(solution)/shard_map/pallas_call | solution.py:522
  144.3 0.7 copy.19
  145.0 2.0 %copy.20 = bf16[1,256,8192]{2,1,0:T(8,128)(2,1)} copy(bf16[1,256,8192]{2,1,0:T(8,128)(2,1)S(1)} %bitcast.10) | data formatting | bytes 8388608
  147.0 0.8 copy.22
  147.8 0.8 copy.23
  148.6 1.3 copy.21
